TPU v7x, 128 devices: a whole 4x4x4 slice. The times are simulated.
128 devices in a mesh: dp: 8 (over z, core), seq: 16 (over y, x).
Axes of the slice: x: 4, y: 4, z: 4, core: 2. Of those that a mesh axis runs over, the one named last changes fastest.
Arguments:
- query_pre: bfloat16 [16, 1024, 6144], P('dp', 'seq'), may hold values from -16 to 16
- key_pre: bfloat16 [16, 1024, 6144], P('dp', 'seq'), may hold values from -16 to 16
- saved_values: bfloat16 [16, 1024, 6144], P('dp', 'seq'), may hold values from -6 to 6
- out_grad: bfloat16 [16, 1024, 6144], P('dp', 'seq'), may hold values from -6 to 6
- out_weight: bfloat16 [6144, 6144], P('seq'), may hold values from -0.078125 to 0.078125
- visible: int32 [16, 1024], P('dp', 'seq'), may hold values from 0 to 4095, as said below
Outputs:
- query_grad: bfloat16 [16, 1024, 6144], P('dp', 'seq')
- key_grad: bfloat16 [16, 1024, 6144], P('dp', 'seq')
- value_grad: bfloat16 [16, 1024, 6144], P('dp', 'seq')
- weight_grad: float32 [6144, 6144], P(('seq', 'dp'))
Inputs may be any that keep to these rules, and one draw needn't show every extreme that they name: `visible`: the 1024 patch numbers of a sample are distinct; 0 and 4095 are among them in every sample.
All inputs are finite; a program needn't handle non-finite values.
Results may differ from a plain program's by a relative error of at most 0.017.
The roundings to bfloat16 on the way count: a program that leaves them out, or rounds other values in their place, can miss the bound.
Values may be sent and summed in bfloat16 or wider, within the bound.
A program may use at most 192 MiB of HBM per device.

v0:
```python
import math

import jax
import jax.numpy as jnp
from jax import lax
from jax.sharding import PartitionSpec as P

HEAD = 128
GRID = 64


def rotation_tables(visible, direction):
    quarter = HEAD // 8
    row_index = (visible // GRID).astype(jnp.float32)
    col_index = (visible % GRID).astype(jnp.float32)
    frequency = jnp.exp(jnp.arange(quarter, dtype=jnp.float32) * (-math.log(100.0) / quarter))
    row_angle = row_index[..., None] * frequency
    col_angle = col_index[..., None] * frequency
    row_cos = jnp.cos(row_angle)
    col_cos = jnp.cos(col_angle)
    row_sin = direction * jnp.sin(row_angle)
    col_sin = direction * jnp.sin(col_angle)
    ones_rest = jnp.ones(row_angle.shape[:-1] + (HEAD - 4 * quarter,), jnp.float32)
    zeros_rest = jnp.zeros(row_angle.shape[:-1] + (HEAD - 4 * quarter,), jnp.float32)
    cos_table = jnp.concatenate([row_cos, row_cos, col_cos, col_cos, ones_rest], axis=-1)
    sin_table = jnp.concatenate([-row_sin, row_sin, -col_sin, col_sin, zeros_rest], axis=-1)
    return (cos_table[:, :, None, :], sin_table[:, :, None, :])


def rotate_tokens(tokens_in, visible, direction):
    seq_count, token_count, model_width = tokens_in.shape
    quarter = HEAD // 8
    split = tokens_in.astype(jnp.float32).reshape(seq_count, token_count, model_width // HEAD, HEAD)
    cos_table, sin_table = rotation_tables(visible, direction)
    paired = split.reshape(seq_count, token_count, model_width // HEAD, 4, 2, quarter)
    partner = paired[:, :, :, :, ::-1, :].reshape(seq_count, token_count, model_width // HEAD, HEAD)
    turned = split * cos_table + partner * sin_table
    return turned.astype(jnp.bfloat16).reshape(seq_count, token_count, model_width)


def attend_forward(query_rows, rotated_key_rows, value_rows):
    score_scale = 1.0 / math.sqrt(query_rows.shape[-1])
    scores = (
        jnp.einsum("rye,cye->yrc", query_rows, rotated_key_rows, preferred_element_type=jnp.float32)
        * score_scale
    )
    row_max = jnp.max(scores, axis=-1, keepdims=True)
    expon = jnp.exp(scores - row_max)
    attention_weights = expon / jnp.sum(expon, axis=-1, keepdims=True)
    attended = jnp.einsum(
        "vly,yvs->lvs",
        attention_weights.astype(jnp.bfloat16),
        value_rows,
        preferred_element_type=jnp.float32,
    ).astype(jnp.bfloat16)
    return (attention_weights, attended)


def attend_backward(
    query_rows, rotated_key_rows, value_rows, attention_weights, attended, output_gradient_rows
):
    score_scale = 1.0 / math.sqrt(query_rows.shape[-1])
    reduced_precision_weights = attention_weights.astype(jnp.bfloat16)
    value_part = jnp.einsum(
        "kqu,qko->uko",
        reduced_precision_weights,
        output_gradient_rows,
        preferred_element_type=jnp.float32,
    ).astype(jnp.bfloat16)
    probability_gradient = jnp.einsum(
        "rye,cye->yrc", output_gradient_rows, value_rows, preferred_element_type=jnp.float32
    )
    row_dot = jnp.sum(
        output_gradient_rows.astype(jnp.float32) * attended.astype(jnp.float32), axis=-1
    )
    score_gradient = (attention_weights * (probability_gradient - row_dot.T[:, :, None])).astype(
        jnp.bfloat16
    )
    query_part = (
        jnp.einsum(
            "vly,yvs->lvs", score_gradient, rotated_key_rows, preferred_element_type=jnp.float32
        )
        * score_scale
    ).astype(jnp.bfloat16)
    key_part = (
        jnp.einsum("kqu,qko->uko", score_gradient, query_rows, preferred_element_type=jnp.float32)
        * score_scale
    ).astype(jnp.bfloat16)
    return (query_part, key_part, value_part)


def body(query_pre, key_pre, saved_values, out_grad, out_weight, visible):
    seq_count, local_tokens, model_width = query_pre.shape
    query_rows = rotate_tokens(query_pre, visible, 1.0)
    rotated_key_rows = rotate_tokens(key_pre, visible, 1.0)
    query_heads, key_heads, value_heads = (
        lax.all_to_all(query_rows, "seq", split_axis=2, concat_axis=1, tiled=True),
        lax.all_to_all(rotated_key_rows, "seq", split_axis=2, concat_axis=1, tiled=True),
        lax.all_to_all(saved_values, "seq", split_axis=2, concat_axis=1, tiled=True),
    )
    seq_length = query_heads.shape[1]
    owned_width = query_heads.shape[2]
    head_count = owned_width // HEAD

    def split_heads(tensor):
        return tensor.reshape(seq_count, seq_length, head_count, HEAD)

    def join_heads(tensor):
        return tensor.reshape(seq_count, seq_length, owned_width)

    query_items = split_heads(query_heads)
    key_items = split_heads(key_heads)
    value_items = split_heads(value_heads)
    attention_weights, attended_items = lax.map(
        lambda operands: attend_forward(*operands), (query_items, key_items, value_items)
    )
    attended = join_heads(attended_items)
    grad_all = lax.all_gather(out_grad, "seq", axis=1, tiled=True)
    output_gradient_rows = jnp.einsum(
        "snd,hd->snh", grad_all, out_weight, preferred_element_type=jnp.float32
    ).astype(jnp.bfloat16)
    weight_grad = lax.psum_scatter(
        jnp.einsum("snh,snd->hd", attended, grad_all, preferred_element_type=jnp.float32).astype(
            jnp.bfloat16
        ),
        "dp",
        scatter_dimension=0,
        tiled=True,
    ).astype(jnp.float32)
    query_part, key_part, value_part = lax.map(
        lambda operands: attend_backward(*operands),
        (
            query_items,
            key_items,
            value_items,
            attention_weights,
            attended_items,
            split_heads(output_gradient_rows),
        ),
    )
    query_back, key_back, value_grad = (
        lax.all_to_all(join_heads(query_part), "seq", split_axis=1, concat_axis=2, tiled=True),
        lax.all_to_all(join_heads(key_part), "seq", split_axis=1, concat_axis=2, tiled=True),
        lax.all_to_all(join_heads(value_part), "seq", split_axis=1, concat_axis=2, tiled=True),
    )
    query_grad = rotate_tokens(query_back, visible, -1.0)
    key_grad = rotate_tokens(key_back, visible, -1.0)
    return (query_grad, key_grad, value_grad, weight_grad)


def solution(mesh):
    in_specs = (
        P("dp", "seq", None),
        P("dp", "seq", None),
        P("dp", "seq", None),
        P("dp", "seq", None),
        P("seq", None),
        P("dp", "seq"),
    )
    out_specs = (
        P("dp", "seq", None),
        P("dp", "seq", None),
        P("dp", "seq", None),
        P(("seq", "dp"), None),
    )
    return jax.shard_map(body, mesh=mesh, in_specs=in_specs, out_specs=out_specs, check_vma=False)
```

profile of v0, /device:TPU:2, one launch (start us, length us, event | category | flops | bytes accessed | tf_op | source)
XLA Modules:
  0.0 509.5 jit_solution(10210333334542132058)
XLA Ops:
  18.7 5.8 %rev.12 = f32[2,64,48,4,2,16]{1,5,4,3,2,0:T(8,128)} reverse(bf16[2,64,48,4,2,16]{1,5,4,3,2,0:T(8,128)(2,1)} %bitcast.248), dimensions={4} | reverse | bytes 4718592 | tf_op jit(solution)/shard_map/rev | solution.py:36
  25.4 8.5 %fusion.69 = (bf16[2,64,6144]{1,2,0:T(8,128)(2,1)}, bf16[2,64,6144]{1,2,0:T(8,128)(2,1)S(1)}) fusion(f32[2,64,48,4,2,16]{1,5,4,3,2,0:T(8,128)} %rev.13, f32[2,64,128]{1,2,0:T(8,128)S(1)} %get-tuple-element.226, f32[2,64,128]{1,2,0:T(8,128)S(1)} %get-tuple-element.225, bf16[2,64,6144]{1,2,0:T(8,128)(2,1)S(1)} %copy.76, f32[2,64,48,4,2,16]{1,5,4,3,2,0:T(8,128)} %rev.12, ...), kind=kLoop, calls=%fused_computation.69 | loop fusion | flops 7864320 | bytes 12713984 | tf_op jit(solution)/shard_map/convert_element_type | solution.py:38
  33.9 26.7 %copy.112 = bf16[2,64,6144]{1,0,2:T(2,128)(2,1)S(1)} copy(bf16[2,64,6144]{1,2,0:T(8,128)(2,1)S(1)} %get-tuple-element.211) | data formatting | bytes 3145728 | tf_op jit(solution)/shard_map/convert_element_type | solution.py:38
  63.8 7.7 %all-to-all-start = ((bf16[16,2,24576]{2,1,0:T(2,128)(2,1)}), bf16[16,2,24576]{2,1,0:T(2,128)(2,1)}, u32[]{:S(2)}, u32[]{:S(2)}) async-start(bf16[16,2,24576]{2,1,0:T(2,128)(2,1)} %reshape.127), calls=%async_computation | async-start | bytes 3145728 | tf_op jit(solution)/shard_map/all_to_all | solution.py:98
  81.8 28.9 %all-to-all-done = bf16[16,2,24576]{2,1,0:T(2,128)(2,1)} async-done(((bf16[16,2,24576]{2,1,0:T(2,128)(2,1)}), bf16[16,2,24576]{2,1,0:T(2,128)(2,1)}, u32[]{:S(2)}, u32[]{:S(2)}) %all-to-all-start) | async-done | bytes 1572896 | tf_op jit(solution)/shard_map/all_to_all | solution.py:98
  110.8 5.6 %all-to-all-start.2 = ((bf16[16,2,24576]{2,1,0:T(2,128)(2,1)}), bf16[16,2,24576]{2,1,0:T(2,128)(2,1)}, u32[]{:S(2)}, u32[]{:S(2)}) async-start(bf16[16,2,24576]{2,1,0:T(2,128)(2,1)} %reshape.131), calls=%async_computation.2 | async-start | bytes 3145728 | tf_op jit(solution)/shard_map/all_to_all | solution.py:99
  116.4 26.8 %copy.111 = bf16[2,64,6144]{1,0,2:T(2,128)(2,1)} copy(bf16[2,64,6144]{1,2,0:T(8,128)(2,1)S(1)} %copy-done.3) | data formatting | bytes 3145728 | tf_op jit(solution)/shard_map/convert_element_type | solution.py:38
  148.1 7.4 %all-to-all-done.2 = bf16[16,2,24576]{2,1,0:T(2,128)(2,1)} async-done(((bf16[16,2,24576]{2,1,0:T(2,128)(2,1)}), bf16[16,2,24576]{2,1,0:T(2,128)(2,1)}, u32[]{:S(2)}, u32[]{:S(2)}) %all-to-all-start.2) | async-done | bytes 1572896 | tf_op jit(solution)/shard_map/all_to_all | solution.py:99
  155.5 5.6 %all-to-all-start.1 = ((bf16[16,2,24576]{2,1,0:T(2,128)(2,1)}), bf16[16,2,24576]{2,1,0:T(2,128)(2,1)}, u32[]{:S(2)}, u32[]{:S(2)}) async-start(bf16[16,2,24576]{2,1,0:T(2,128)(2,1)} %reshape.129), calls=%async_computation.1 | async-start | bytes 3145728 | tf_op jit(solution)/shard_map/all_to_all | solution.py:97
  216.7 55.5 %while.26 = (s32[]{:T(128)}, f32[2,3,1024,1024]{2,3,1,0:T(8,128)}, bf16[2,1024,3,128]{1,3,2,0:T(8,128)(2,1)S(1)}, bf16[2,1024,3,128]{3,1,2,0:T(8,128)(2,1)}, bf1...) while((s32[]{:T(128)}, f32[2,3,1024,1024]{2,3,1,0:T(8,128)}, ...), condition=%wide.region_3.4_spmd, body=%wide.region_0.3_spmd.sunk | while | flops 1629881344 | bytes 59811956 | solution.py:114
  216.7 9.8 %fusion.129 = (f32[3,1024]{1,0:T(4,128)S(1)}, f32[3,1024,1024]{1,2,0:T(8,128)}) fusion(bf16[2,1024,3,128]{3,1,2,0:T(8,128)(2,1)} %get-tuple-element.351, s32[]{:T(128)S(6)} %copy.138, bf16[2,1024,3,128]{3,1,2,0:T(8,128)(2,1)} %get-tuple-element.350), kind=kOutput, calls=%fused_computation.114.clone.1 | convolution fusion | flops 814744576 | bytes 14169088 | tf_op jit(solution)/shard_map/while/body/eval_jaxpr/sub | solution.py:48
  226.5 12.3 %bitcast_dynamic-update-slice_fusion.2 = f32[2,3,1024,1024]{2,3,1,0:T(8,128)} fusion(f32[2,3,1024,1024]{2,3,1,0:T(8,128)} %get-tuple-element.341, s32[]{:T(128)S(6)} %copy.138, f32[3,1024,1024]{1,2,0:T(8,128)} %get-tuple-element.319, f32[3,1024]{1,0:T(4,128)S(1)} %get-tuple-element.320), kind=kLoop, calls=%fused_computation.1.clone.1 | loop fusion | flops 3145728 | bytes 25178116 | tf_op jit(solution)/shard_map/while/body/jit(dynamic_update_index_in_dim)/dynamic_update_slice | solution.py:114
  238.9 5.6 %fusion.130 = bf16[2,1024,3,128]{1,3,2,0:T(8,128)(2,1)S(1)} fusion(bf16[2,1024,3,128]{1,3,2,0:T(8,128)(2,1)S(1)} %get-tuple-element.342, s32[]{:T(128)S(6)} %copy.138, f32[3,1024,1024]{1,2,0:T(8,128)} %get-tuple-element.319, f32[3,1024]{1,0:T(4,128)S(1)} %get-tuple-element.320, bf16[2,1024,3,128]{1,3,2,0:T(8,128)(2,1)S(1)} %copy-done.11), kind=kOutput, calls=%fused_computation.12.clone.1 | convolution fusion | flops 811991040 | bytes 14173184 | tf_op jit(solution)/shard_map/while/body/eval_jaxpr/vly,yvs->lvs/dot_general | solution.py:50
  244.5 9.8 %fusion.129 = (f32[3,1024]{1,0:T(4,128)S(1)}, f32[3,1024,1024]{1,2,0:T(8,128)}) fusion(bf16[2,1024,3,128]{3,1,2,0:T(8,128)(2,1)} %get-tuple-element.351, s32[]{:T(128)S(6)} %copy.138, bf16[2,1024,3,128]{3,1,2,0:T(8,128)(2,1)} %get-tuple-element.350), kind=kOutput, calls=%fused_computation.114.clone.1 | convolution fusion | flops 814744576 | bytes 14169088 | tf_op jit(solution)/shard_map/while/body/eval_jaxpr/sub | solution.py:48
  254.3 12.2 %bitcast_dynamic-update-slice_fusion.2 = f32[2,3,1024,1024]{2,3,1,0:T(8,128)} fusion(f32[2,3,1024,1024]{2,3,1,0:T(8,128)} %get-tuple-element.341, s32[]{:T(128)S(6)} %copy.138, f32[3,1024,1024]{1,2,0:T(8,128)} %get-tuple-element.319, f32[3,1024]{1,0:T(4,128)S(1)} %get-tuple-element.320), kind=kLoop, calls=%fused_computation.1.clone.1 | loop fusion | flops 3145728 | bytes 25178116 | tf_op jit(solution)/shard_map/while/body/jit(dynamic_update_index_in_dim)/dynamic_update_slice | solution.py:114
  266.6 5.6 %fusion.130 = bf16[2,1024,3,128]{1,3,2,0:T(8,128)(2,1)S(1)} fusion(bf16[2,1024,3,128]{1,3,2,0:T(8,128)(2,1)S(1)} %get-tuple-element.342, s32[]{:T(128)S(6)} %copy.138, f32[3,1024,1024]{1,2,0:T(8,128)} %get-tuple-element.319, f32[3,1024]{1,0:T(4,128)S(1)} %get-tuple-element.320, bf16[2,1024,3,128]{1,3,2,0:T(8,128)(2,1)S(1)} %copy-done.11), kind=kOutput, calls=%fused_computation.12.clone.1 | convolution fusion | flops 811991040 | bytes 14173184 | tf_op jit(solution)/shard_map/while/body/eval_jaxpr/vly,yvs->lvs/dot_general | solution.py:50
  272.2 16.7 %bitcast_convert_fusion.8 = bf16[384,6144]{1,0:T(8,128)(2,1)} fusion(bf16[2,1024,384]{1,2,0:T(8,128)(2,1)S(1)} %bitcast.249, bf16[2,1024,6144]{2,1,0:T(8,128)(2,1)} %all-gather.2.cloned.1.call-done), kind=kOutput, calls=%fused_computation.65 | convolution fusion | flops 9666035712 | bytes 31457280 | tf_op jit(solution)/shard_map/snh,snd->hd/dot_general | solution.py:123
  289.0 16.1 %fusion.76 = bf16[2,1024,384]{1,2,0:T(8,128)(2,1)S(1)} fusion(bf16[2,1024,6144]{2,1,0:T(8,128)(2,1)} %all-gather.2.cloned.1.call-done, bf16[384,6144]{1,0:T(8,128)(2,1)} %param.14), kind=kOutput, calls=%fused_computation.78 | convolution fusion | flops 9664462848 | bytes 31457280 | tf_op jit(solution)/shard_map/snd,hd->snh/dot_general | solution.py:119
  309.1 86.6 %while.27 = (s32[]{:T(128)}, bf16[2,1024,3,128]{1,3,2,0:T(8,128)(2,1)}, bf16[2,1024,3,128]{1,3,2,0:T(8,128)(2,1)}, bf16[2,1024,3,128]{1,3,2,0:T(8,128)(2,1)}, bf...) while((s32[]{:T(128)}, ...), condition=%wide.region_6.7_spmd, body=%wide.region_4.6_spmd.sunk | while | flops 3233805312 | bytes 184058288 | solution.py:130
  309.3 12.1 %constant_dynamic-slice_fusion.7 = f32[1,3,1024,1024]{2,3,1,0:T(8,128)} fusion(f32[2,3,1024,1024]{2,3,1,0:T(8,128)} %get-tuple-element.381, s32[]{:T(128)S(6)} %copy.148), kind=kLoop, calls=%fused_computation.55.clone.1 | loop fusion | bytes 25165828 | tf_op jit(solution)/shard_map/while/body/jit(dynamic_index_in_dim)/dynamic_slice | solution.py:130
  321.4 12.7 %copy.116 = f32[1,3,1024,1024]{3,2,1,0:T(8,128)} copy(f32[1,3,1024,1024]{2,3,1,0:T(8,128)} %constant_dynamic-slice_fusion.7) | data formatting | bytes 25165824 | tf_op jit(solution)/shard_map/while/body/jit(dynamic_index_in_dim)/dynamic_slice | solution.py:130
  339.4 6.3 %fusion.140 = bf16[3,1024,1024]{2,1,0:T(8,128)(2,1)S(1)} fusion(f32[1,3,1024,1024]{3,2,1,0:T(8,128)} %copy.116, f32[3,1024]{1,0:T(4,128)} %bitcast.265, bf16[2,1024,3,128]{3,1,2,0:T(8,128)(2,1)} %get-tuple-element.383, s32[]{:T(128)S(6)} %copy.148, bf16[2,1024,3,128]{1,3,2,0:T(8,128)(2,1)S(1)} %get-tuple-element.382), kind=kOutput, calls=%fused_computation.30.clone.1 | convolution fusion | flops 814743552 | bytes 20464640 | tf_op jit(solution)/shard_map/while/body/eval_jaxpr/rye,cye->yrc/dot_general | solution.py:70
  352.7 11.8 %constant_dynamic-slice_fusion.7 = f32[1,3,1024,1024]{2,3,1,0:T(8,128)} fusion(f32[2,3,1024,1024]{2,3,1,0:T(8,128)} %get-tuple-element.381, s32[]{:T(128)S(6)} %copy.148), kind=kLoop, calls=%fused_computation.55.clone.1 | loop fusion | bytes 25165828 | tf_op jit(solution)/shard_map/while/body/jit(dynamic_index_in_dim)/dynamic_slice | solution.py:130
  364.5 12.7 %copy.116 = f32[1,3,1024,1024]{3,2,1,0:T(8,128)} copy(f32[1,3,1024,1024]{2,3,1,0:T(8,128)} %constant_dynamic-slice_fusion.7) | data formatting | bytes 25165824 | tf_op jit(solution)/shard_map/while/body/jit(dynamic_index_in_dim)/dynamic_slice | solution.py:130
  382.4 6.3 %fusion.140 = bf16[3,1024,1024]{2,1,0:T(8,128)(2,1)S(1)} fusion(f32[1,3,1024,1024]{3,2,1,0:T(8,128)} %copy.116, f32[3,1024]{1,0:T(4,128)} %bitcast.265, bf16[2,1024,3,128]{3,1,2,0:T(8,128)(2,1)} %get-tuple-element.383, s32[]{:T(128)S(6)} %copy.148, bf16[2,1024,3,128]{1,3,2,0:T(8,128)(2,1)S(1)} %get-tuple-element.382), kind=kOutput, calls=%fused_computation.30.clone.1 | convolution fusion | flops 814743552 | bytes 20464640 | tf_op jit(solution)/shard_map/while/body/eval_jaxpr/rye,cye->yrc/dot_general | solution.py:70
  408.6 17.1 %all-to-all-done.4 = bf16[2,1024,384]{2,0,1:T(2,128)(2,1)S(1)} async-done(((bf16[2,1024,384]{2,0,1:T(2,128)(2,1)}), bf16[2,1024,384]{2,0,1:T(2,128)(2,1)S(1)}, u32[]{:S(2)}, u32[]{:S(2)}) %all-to-all-start.4) | async-done | bytes 1572896 | tf_op jit(solution)/shard_map/all_to_all | solution.py:143
  425.7 5.3 %all-to-all-start.3 = ((bf16[2,1024,384]{2,0,1:T(2,128)(2,1)}), bf16[2,1024,384]{2,0,1:T(2,128)(2,1)S(1)}, u32[]{:S(2)}, u32[]{:S(2)}) async-start(bf16[2,1024,384]{2,0,1:T(2,128)(2,1)} %copy.90), calls=%async_computation.3 | async-start | bytes 3145728 | tf_op jit(solution)/shard_map/all_to_all | solution.py:142
  436.1 15.0 %all-to-all-done.3 = bf16[2,1024,384]{2,0,1:T(2,128)(2,1)S(1)} async-done(((bf16[2,1024,384]{2,0,1:T(2,128)(2,1)}), bf16[2,1024,384]{2,0,1:T(2,128)(2,1)S(1)}, u32[]{:S(2)}, u32[]{:S(2)}) %all-to-all-start.3) | async-done | bytes 1572896 | tf_op jit(solution)/shard_map/all_to_all | solution.py:142
  451.1 6.4 %all-to-all-start.5 = ((bf16[2,1024,384]{2,0,1:T(2,128)(2,1)}), bf16[2,1024,384]{2,0,1:T(2,128)(2,1)}, u32[]{:S(2)}, u32[]{:S(2)}) async-start(bf16[2,1024,384]{2,0,1:T(2,128)(2,1)} %copy.98), calls=%async_computation.5 | async-start | bytes 3145728 | tf_op jit(solution)/shard_map/all_to_all | solution.py:144
  462.4 6.3 %rev.15 = f32[2,64,48,4,2,16]{1,5,4,3,2,0:T(8,128)} reverse(f32[2,64,48,4,2,16]{1,5,4,3,2,0:T(8,128)} %bitcast.245), dimensions={4} | reverse | bytes 6291456 | tf_op jit(solution)/shard_map/rev | solution.py:36
  473.4 6.2 %rev.14 = f32[2,64,48,4,2,16]{1,5,4,3,2,0:T(8,128)} reverse(f32[2,64,48,4,2,16]{1,5,4,3,2,0:T(8,128)} %bitcast.246), dimensions={4} | reverse | bytes 6291456 | tf_op jit(solution)/shard_map/rev | solution.py:36
  479.6 10.8 %fusion.73 = (bf16[2,64,6144]{1,2,0:T(8,128)(2,1)S(1)}, bf16[2,64,6144]{1,2,0:T(8,128)(2,1)}) fusion(f32[2,64,48,4,2,16]{1,5,4,3,2,0:T(8,128)} %rev.15, f32[2,64,16,384]{1,3,2,0:T(8,128)} %copy.96, f32[2,64,128]{1,2,0:T(8,128)S(1)} %constant_dynamic-update-slice_fusion.10, f32[2,64,128]{1,2,0:T(8,128)S(1)} %copy-done.14, f32[2,64,48,4,2,16]{1,5,4,3,2,0:T(8,128)} %rev.14, ...), kind=kLoop, calls=%fused_computation.73 | loop fusion | flops 6291456 | bytes 15859712 | tf_op jit(solution)/shard_map/convert_element_type | solution.py:38
  (137 shorter events, 154.0 us)
Async XLA Ops:
  7.2 265.1 %all-gather.2.cloned.1.call-start = ((), (), s32[]{:S(2)}) async-start(), calls=%async_computation.7 | async-start | bytes 26738688 | tf_op jit(solution)/shard_map/all_gather | solution.py:118
  18.7 5.9 %copy-start.17 = (s32[2,64]{1,0:T(2,128)S(1)}, s32[2,64]{1,0:T(2,128)}, u32[]{:S(2)}) copy-start(s32[2,64]{1,0:T(2,128)} %param.15) | copy-start | bytes 1540
  25.2 8.7 %copy-start.15 = (f32[2,64,128]{1,2,0:T(8,128)}, f32[2,64,128]{1,2,0:T(8,128)S(1)}, u32[]{:S(2)}) copy-start(f32[2,64,128]{1,2,0:T(8,128)S(1)} %get-tuple-element.212) | copy-start | bytes 196612
  25.4 8.5 %copy-start.13 = (f32[2,64,128]{1,2,0:T(8,128)}, f32[2,64,128]{1,2,0:T(8,128)S(1)}, u32[]{:S(2)}) copy-start(f32[2,64,128]{1,2,0:T(8,128)S(1)} %get-tuple-element.225) | copy-start | bytes 196612
  63.8 7.7 %copy-start.12 = (bf16[2,64,6144]{2,1,0:T(8,128)(2,1)S(1)}, bf16[2,64,6144]{2,1,0:T(8,128)(2,1)}, u32[]{:S(2)}) copy-start(bf16[2,64,6144]{2,1,0:T(8,128)(2,1)} %param.12) | copy-start | bytes 4718596
  63.8 47.0 %all-to-all-start = ((bf16[16,2,24576]{2,1,0:T(2,128)(2,1)}), bf16[16,2,24576]{2,1,0:T(2,128)(2,1)}, u32[]{:S(2)}, u32[]{:S(2)}) async-start(bf16[16,2,24576]{2,1,0:T(2,128)(2,1)} %reshape.127), calls=%async_computation | async-start | bytes 3145728 | tf_op jit(solution)/shard_map/all_to_all | solution.py:98
  76.7 39.7 %copy-start.3 = (bf16[2,64,6144]{1,2,0:T(8,128)(2,1)S(1)}, bf16[2,64,6144]{1,2,0:T(8,128)(2,1)}, u32[]{:S(2)}) copy-start(bf16[2,64,6144]{1,2,0:T(8,128)(2,1)} %get-tuple-element.210) | copy-start | bytes 4718596
  110.8 44.7 %all-to-all-start.2 = ((bf16[16,2,24576]{2,1,0:T(2,128)(2,1)}), bf16[16,2,24576]{2,1,0:T(2,128)(2,1)}, u32[]{:S(2)}, u32[]{:S(2)}) async-start(bf16[16,2,24576]{2,1,0:T(2,128)(2,1)} %reshape.131), calls=%async_computation.2 | async-start | bytes 3145728 | tf_op jit(solution)/shard_map/all_to_all | solution.py:99
  155.5 44.4 %all-to-all-start.1 = ((bf16[16,2,24576]{2,1,0:T(2,128)(2,1)}), bf16[16,2,24576]{2,1,0:T(2,128)(2,1)}, u32[]{:S(2)}, u32[]{:S(2)}) async-start(bf16[16,2,24576]{2,1,0:T(2,128)(2,1)} %reshape.129), calls=%async_computation.1 | async-start | bytes 3145728 | tf_op jit(solution)/shard_map/all_to_all | solution.py:97
  161.1 338.9 %reduce-scatter.2.cloned.1.call-start = ((), (), s32[]{:S(2)}) async-start(), calls=%async_computation.8 | async-start | bytes 5308416 | tf_op jit(solution)/shard_map/reduce_scatter | solution.py:122
  226.5 12.3 %copy-start.11 = (bf16[2,1024,3,128]{1,3,2,0:T(8,128)(2,1)S(1)}, bf16[2,1024,3,128]{1,3,2,0:T(8,128)(2,1)}, u32[]{:S(2)}) copy-start(bf16[2,1024,3,128]{1,3,2,0:T(8,128)(2,1)} %get-tuple-element.352) | copy-start | bytes 4718596 | tf_op jit(solution)/shard_map/while
  254.3 12.3 %copy-start.11 = (bf16[2,1024,3,128]{1,3,2,0:T(8,128)(2,1)S(1)}, bf16[2,1024,3,128]{1,3,2,0:T(8,128)(2,1)}, u32[]{:S(2)}) copy-start(bf16[2,1024,3,128]{1,3,2,0:T(8,128)(2,1)} %get-tuple-element.352) | copy-start | bytes 4718596 | tf_op jit(solution)/shard_map/while
  272.2 16.7 %copy-start.1 = (bf16[2,1024,3,128]{1,3,2,0:T(8,128)(2,1)}, bf16[2,1024,3,128]{1,3,2,0:T(8,128)(2,1)S(1)}, u32[]{:S(2)}) copy-start(bf16[2,1024,3,128]{1,3,2,0:T(8,128)(2,1)S(1)} %get-tuple-element.362) | copy-start | bytes 4718596
  339.4 6.3 %copy-start.2 = (bf16[2,1024,3,128]{1,3,2,0:T(8,128)(2,1)S(1)}, bf16[2,1024,3,128]{1,3,2,0:T(8,128)(2,1)}, u32[]{:S(2)}) copy-start(bf16[2,1024,3,128]{1,3,2,0:T(8,128)(2,1)} %get-tuple-element.380) | copy-start | bytes 4718596 | tf_op jit(solution)/shard_map/while
  339.4 10.5 %slice-start = ((s8[12582912]{0:T(1024)(128)(4,1)}), s8[4194304]{0:T(1024)(128)(4,1)S(1)}, s32[]{:S(2)}) async-start(s8[12582912]{0:T(1024)(128)(4,1)} %bitcast.242), calls=%async_computation.9 | async-start | bytes 8388608 | tf_op jit(solution)/shard_map/while
  339.4 10.5 %slice-start.1 = ((s8[12582912]{0:T(1024)(128)(4,1)}), s8[4194304]{0:T(1024)(128)(4,1)S(1)}, s32[]{:S(2)}) async-start(s8[12582912]{0:T(1024)(128)(4,1)} %bitcast.242), calls=%async_computation.10 | async-start | bytes 8388608 | tf_op jit(solution)/shard_map/while
  345.7 3.1 copy-start
  345.7 4.2 slice-start.2
  382.4 6.3 %copy-start.2 = (bf16[2,1024,3,128]{1,3,2,0:T(8,128)(2,1)S(1)}, bf16[2,1024,3,128]{1,3,2,0:T(8,128)(2,1)}, u32[]{:S(2)}) copy-start(bf16[2,1024,3,128]{1,3,2,0:T(8,128)(2,1)} %get-tuple-element.380) | copy-start | bytes 4718596 | tf_op jit(solution)/shard_map/while
  382.4 10.5 %slice-start = ((s8[12582912]{0:T(1024)(128)(4,1)}), s8[4194304]{0:T(1024)(128)(4,1)S(1)}, s32[]{:S(2)}) async-start(s8[12582912]{0:T(1024)(128)(4,1)} %bitcast.242), calls=%async_computation.9 | async-start | bytes 8388608 | tf_op jit(solution)/shard_map/while
  382.4 10.5 %slice-start.1 = ((s8[12582912]{0:T(1024)(128)(4,1)}), s8[4194304]{0:T(1024)(128)(4,1)S(1)}, s32[]{:S(2)}) async-start(s8[12582912]{0:T(1024)(128)(4,1)} %bitcast.242), calls=%async_computation.10 | async-start | bytes 8388608 | tf_op jit(solution)/shard_map/while
  388.7 3.1 copy-start
  388.7 3.1 copy-start.7
  388.8 4.2 slice-start.2
  395.7 10.0 %copy-start.6 = (bf16[2,1024,3,128]{1,3,2,0:T(8,128)(2,1)S(1)}, bf16[2,1024,3,128]{1,3,2,0:T(8,128)(2,1)}, u32[]{:S(2)}) copy-start(bf16[2,1024,3,128]{1,3,2,0:T(8,128)(2,1)} %get-tuple-element.93) | copy-start | bytes 4718596
  400.8 24.9 %all-to-all-start.4 = ((bf16[2,1024,384]{2,0,1:T(2,128)(2,1)}), bf16[2,1024,384]{2,0,1:T(2,128)(2,1)S(1)}, u32[]{:S(2)}, u32[]{:S(2)}) async-start(bf16[2,1024,384]{2,0,1:T(2,128)(2,1)} %copy.94), calls=%async_computation.4 | async-start | bytes 3145728 | tf_op jit(solution)/shard_map/all_to_all | solution.py:143
  425.7 25.4 %all-to-all-start.3 = ((bf16[2,1024,384]{2,0,1:T(2,128)(2,1)}), bf16[2,1024,384]{2,0,1:T(2,128)(2,1)S(1)}, u32[]{:S(2)}, u32[]{:S(2)}) async-start(bf16[2,1024,384]{2,0,1:T(2,128)(2,1)} %copy.90), calls=%async_computation.3 | async-start | bytes 3145728 | tf_op jit(solution)/shard_map/all_to_all | solution.py:142
  431.0 26.4 %copy-start.16 = (f32[2,64,128]{1,2,0:T(8,128)S(1)}, f32[2,64,128]{1,2,0:T(8,128)}, u32[]{:S(2)}) copy-start(f32[2,64,128]{1,2,0:T(8,128)} %copy-done.15) | copy-start | bytes 196612
  451.1 6.6 %copy-start.4 = (bf16[2,1024,384]{2,0,1:T(2,128)(2,1)}, bf16[2,1024,384]{2,0,1:T(2,128)(2,1)S(1)}, u32[]{:S(2)}) copy-start(bf16[2,1024,384]{2,0,1:T(2,128)(2,1)S(1)} %all-to-all-done.3) | copy-start | bytes 4718596
  451.1 45.9 %all-to-all-start.5 = ((bf16[2,1024,384]{2,0,1:T(2,128)(2,1)}), bf16[2,1024,384]{2,0,1:T(2,128)(2,1)}, u32[]{:S(2)}, u32[]{:S(2)}) async-start(bf16[2,1024,384]{2,0,1:T(2,128)(2,1)} %copy.98), calls=%async_computation.5 | async-start | bytes 3145728 | tf_op jit(solution)/shard_map/all_to_all | solution.py:144
  462.4 6.3 %copy-start.5 = (bf16[2,1024,384]{2,0,1:T(2,128)(2,1)S(1)}, bf16[2,1024,384]{2,0,1:T(2,128)(2,1)}, u32[]{:S(2)}) copy-start(bf16[2,1024,384]{2,0,1:T(2,128)(2,1)} %copy-done.4) | copy-start | bytes 4718596
  473.4 6.2 %copy-start.14 = (f32[2,64,128]{1,2,0:T(8,128)S(1)}, f32[2,64,128]{1,2,0:T(8,128)}, u32[]{:S(2)}) copy-start(f32[2,64,128]{1,2,0:T(8,128)} %copy-done.13) | copy-start | bytes 196612
  (7 other events, 11.9 us)
Sparse Core Ops, SparseCore 0:
  10.1 206.9 all-gather.1
  289.1 38.1 reduce-scatter.1
where the time goes:
time: 520 us; the launch traced here: 509 us
  local copies, waits for them, and re-layouts  248 us (48%)
  matrix products  86.5 us (17%)
  waiting for transfers between devices  74.4 us (14%)
  other arithmetic  49.7 us (10%)
  starting transfers between devices  35.7 us (7%)
  between operations  14.8 us (3%)
    convert_element_type x2, local copies, waits for them, and re-layouts, rotate_tokens(): turned.astype(jnp.bfloat16).reshape(seq_count, token_count, model_width)  53.4 us
    dynamic_slice x4, local copies, waits for them, and re-layouts, body(): lax.map(lambda operands: attend_backward(*operands), (query_items, key_it...  49.4 us
    unnamed x33, local copies, waits for them, and re-layouts  43.7 us
    all_to_all x1, waiting for transfers between devices, body(): lax.all_to_all(rotated_key_rows, 'seq', split_axis=2, concat_axis=1, tile...  28.9 us
    dynamic_update_slice x2, other arithmetic, body(): lax.map(lambda operands: attend_forward(*operands), (query_items, key_ite...  24.6 us
    rev x4, local copies, waits for them, and re-layouts, rotate_tokens(): paired[:, :, :, :, ::-1, :]  21.9 us
    sub x2, matrix products, attend_forward(): expon = jnp.exp(scores - row_max)  19.6 us
    convert_element_type x2, other arithmetic, rotate_tokens(): turned.astype(jnp.bfloat16).reshape(seq_count, token_count, model_width)  19.2 us
  transfers between devices with their start and end apart: 8, of which 5 were waited for; matrix products, arithmetic and copies ran while one was open for 71% of the time, Pallas kernels for 0%

commit v1 on v0

v1 whole, which is shorter than its diff:
```python
import functools
import math

import jax
import jax.numpy as jnp
from jax import lax
from jax.experimental import pallas as pl
from jax.experimental.pallas import tpu as pltpu
from jax.sharding import PartitionSpec as P

HEAD = 128
GRID = 64
SIDE = 4
GROUP = SIDE * SIDE
MESH = pl.DeviceIdType.MESH
F32 = jnp.float32
BF16 = jnp.bfloat16
MIB = 1024 * 1024
NT = (((1,), (1,)), ((), ()))
TN = (((0,), (0,)), ((), ()))


def dot(a, b, dims=(((1,), (0,)), ((), ()))):
    return lax.dot_general(a, b, dims, preferred_element_type=F32)


def turn(x, cosine, sine):
    lane = lax.broadcasted_iota(jnp.int32, x.shape, 1)
    quarter = HEAD // 8
    ahead = pltpu.roll(x, HEAD - quarter, 1)
    behind = pltpu.roll(x, quarter, 1)
    partner = jnp.where((lane // quarter) % 2 == 0, ahead, behind)
    return x * cosine + partner * sine


def remote(src, dst, send, recv, target):
    return pltpu.make_async_remote_copy(
        src_ref=src,
        dst_ref=dst,
        send_sem=send,
        recv_sem=recv,
        device_id={"seq": target},
        device_id_type=MESH,
    )


def enter(me):
    barrier = pltpu.get_barrier_semaphore()

    def greet(off, carry):
        pl.semaphore_signal(
            barrier, inc=1, device_id={"seq": lax.rem(me + off, GROUP)}, device_id_type=MESH
        )
        return carry

    lax.fori_loop(1, GROUP, greet, 0)
    pl.semaphore_wait(barrier, GROUP - 1)


def rows_of(block, size):
    return pl.ds(pl.multiple_of(block * size, size), size)


def gather_kernel(
    q_in, k_in, v_in, g_in, w_in, vis_in, pos_in,
    q_out, k_out, v_out, do_out, att_out, lse_out, cos_out, sin_out, wg_out,
    qb, kb, vb, gb, wb, visb, cosb, sinb, att, dot_t, lse, acc, stage,
    a2a_send, a2a_recv, ag_send, ag_recv, local_sem, out_sem,
):
    me = lax.axis_index("seq")
    px, py = lax.rem(me, SIDE), lax.div(me, SIDE)
    samples, local = q_in.shape[0], q_in.shape[1]
    width = q_in.shape[2] // GROUP
    heads = width // HEAD
    tokens = local * GROUP
    part = tokens // SIDE
    model = g_in.shape[2]
    scale = math.log2(math.e) / math.sqrt(HEAD)

    def at(axis, delta, axis2=None, delta2=0):
        x, y = px, py
        for a, d in ((axis, delta), (axis2, delta2)):
            if a == 0:
                x = lax.rem(x + d, SIDE)
            elif a == 1:
                y = lax.rem(y + d, SIDE)
        return y * SIDE + x

    local_copies = [
        pltpu.make_async_copy(w_in, wb, local_sem.at[0]),
        pltpu.make_async_copy(g_in, gb.at[:, rows_of(me, local), :], local_sem.at[1]),
        pltpu.make_async_copy(vis_in, visb.at[me], local_sem.at[2]),
    ]
    for t, (src, dst) in enumerate(((q_in, qb), (k_in, kb), (v_in, vb))):
        local_copies.append(
            pltpu.make_async_copy(
                src.at[:, :, rows_of(me, width)], dst.at[:, rows_of(me, local), :], local_sem.at[3 + t]
            )
        )
    for copy in local_copies:
        copy.start()

    enter(me)

    dirs = (1, SIDE - 1)
    mid = local // 2

    def half_rows(block, which):
        return pl.ds(pl.multiple_of(block * local + which * mid, mid), mid)

    def ag_copy(half, slot, direction, stage_index, block, axis, from_input=False):
        if stage_index == 0:
            place = rows_of(block, local)
        else:
            place = half_rows(block, direction)
        dst = gb.at[half, place, :]
        src = g_in.at[half] if from_input else dst
        return remote(
            src, dst,
            ag_send.at[half, slot, direction, stage_index],
            ag_recv.at[half, slot, direction, stage_index],
            at(axis, dirs[direction]),
        )

    started = []

    def begin(*args, **kwargs):
        copy = ag_copy(*args, **kwargs)
        copy.start()
        started.append(copy)

    def first_direct(half, direction):
        begin(half, 0, direction, 0, me, half, from_input=True)

    def second_direct(half, b):
        for direction in range(2):
            begin(half, 1 + b, direction, 0, at(half, b), 1 - half, from_input=b == 0)

    def got_first(half, direction):
        block = at(half, SIDE - dirs[direction])
        ag_copy(half, 0, direction, 0, block, half).wait_recv()
        begin(half, 0, direction, 1, block, half)
        second_direct(half, (SIDE - dirs[direction]) % SIDE)

    def got_first_far(half):
        block = at(half, 2)
        for direction in range(2):
            ag_copy(half, 0, direction, 1, block, half).wait_recv()
        second_direct(half, 2)

    def got_second(half, b):
        for direction in range(2):
            block = at(half, b, 1 - half, SIDE - dirs[direction])
            ag_copy(half, 1 + b, direction, 0, block, 1 - half).wait_recv()
            begin(half, 1 + b, direction, 1, block, 1 - half)

    def got_second_far(half, b):
        block = at(half, b, 1 - half, 2)
        for direction in range(2):
            ag_copy(half, 1 + b, direction, 1, block, 1 - half).wait_recv()

    for half in range(2):
        for direction in range(2):
            first_direct(half, direction)
    for half in range(2):
        second_direct(half, 0)

    pairs = ((q_in, qb), (k_in, kb), (v_in, vb))

    def send_vis(off, carry):
        target = lax.rem(me + off, GROUP)
        remote(vis_in, visb.at[me], a2a_send.at[3], a2a_recv.at[3], target).start()
        return carry

    lax.fori_loop(1, GROUP, send_vis, 0)
    for t, (src, dst) in enumerate(pairs):

        def send_one(off, carry, src=src, dst=dst, t=t):
            target = lax.rem(me + off, GROUP)
            remote(
                src.at[:, :, rows_of(target, width)],
                dst.at[:, rows_of(me, local), :],
                a2a_send.at[t], a2a_recv.at[t], target,
            ).start()
            return carry

        lax.fori_loop(1, GROUP, send_one, 0)

    def a2a_wait(t, sem, ref):
        view = ref.at[:, pl.ds(0, tokens - local), :] if t < 3 else ref.at[pl.ds(0, GROUP - 1)]
        pltpu.make_async_copy(view, view, sem.at[t]).wait()

    for copy in local_copies:
        copy.wait()

    for half in range(2):
        for direction in range(2):
            got_first(half, direction)
    for half in range(2):
        got_second(half, 0)

    a2a_wait(3, a2a_recv, visb)

    def tables(src, carry):
        seen = visb[src, 0:1, :]
        row, col = lax.div(seen, GRID), lax.rem(seen, GRID)
        place = lax.broadcasted_iota(jnp.int32, (HEAD, 2 * local), 0)
        hot = jnp.where((place == row) | (place == col + GRID), 1.0, 0.0)
        both = lax.dot_general(
            hot, pos_in[...], TN, preferred_element_type=F32, precision=lax.Precision.HIGHEST
        )
        for s in range(samples):
            rows = both[s * local:(s + 1) * local]
            cosb[s, rows_of(src, local), :] = rows[:, :HEAD]
            sinb[s, rows_of(src, local), :] = rows[:, HEAD:]
        return carry

    lax.fori_loop(0, GROUP, tables, 0)
    for t, (_, dst) in enumerate(pairs):
        a2a_wait(t, a2a_recv, dst)

    chunk = 256

    def forward(s, h):
        lanes = slice(h * HEAD, (h + 1) * HEAD)
        cosine, sine = cosb[s], sinb[s]
        qb[s, :, lanes] = turn(qb[s, :, lanes].astype(F32), cosine, sine).astype(BF16)
        kb[s, :, lanes] = turn(kb[s, :, lanes].astype(F32), cosine, sine).astype(BF16)
        values_t = vb[s, :, lanes].astype(F32).T.astype(BF16)

        def one(c, carry):
            place = rows_of(c, chunk)
            scores = dot(kb[s, :, lanes], qb[s, place, lanes], NT) * scale
            top = jnp.max(scores, axis=0, keepdims=True)
            expon = jnp.exp2(scores - top)
            total = jnp.sum(expon, axis=0, keepdims=True)
            probs = (expon * (1.0 / total)).astype(BF16)
            att[s, lanes, place] = dot(values_t, probs).astype(BF16)
            lse[s * heads + h:s * heads + h + 1, place] = top + jnp.log2(total)
            return carry

        lax.fori_loop(0, tokens // chunk, one, 0)

    def out_dir(s, row):
        place = rows_of(row, part)
        dot_t[s, :, place] = dot(wb[...], gb[s, place, :], NT).astype(BF16)

    tile = stage.shape[2]

    def weight_part(row, first=False, last=False):
        place = rows_of(row, part)

        def put(j, slot):
            return pltpu.make_async_copy(
                stage.at[slot], wg_out.at[:, rows_of(j, tile)], out_sem.at[slot]
            )

        def one(j, carry):
            cols = rows_of(j, tile)
            total = dot(att[0, :, place], gb[0, place, cols])
            for s in range(1, samples):
                total += dot(att[s, :, place], gb[s, place, cols])
            if not first:
                total += acc[:, cols]
            if last:
                slot = lax.rem(j, 2)

                @pl.when(j >= 2)
                def _():
                    put(j - 2, slot).wait()

                stage[slot] = total.astype(BF16)
                put(j, slot).start()
            else:
                acc[:, cols] = total
            return carry

        steps = model // tile
        lax.fori_loop(0, steps, one, 0)
        if last:
            for j in (steps - 2, steps - 1):
                put(j, j % 2).wait()

    near = [lax.rem(py + d, SIDE) for d in range(SIDE)]

    forward(0, 0)
    for half in range(2):
        got_first_far(half)
    forward(0, 1)
    for b in (1, SIDE - 1):
        for half in range(2):
            got_second(half, b)
        forward(*((0, 2) if b == 1 else (1, 0)))
    for half in range(2):
        got_second_far(half, 0)
    out_dir(0, near[0])
    out_dir(1, near[0])
    for half in range(2):
        got_second(half, 2)
    forward(1, 1)
    forward(1, 2)
    weight_part(near[0], first=True)
    for b in (1, SIDE - 1):
        for half in range(2):
            got_second_far(half, b)
        out_dir(0, near[b])
        out_dir(1, near[b])
        weight_part(near[b])
    outs = [
        pltpu.make_async_copy(src, dst, out_sem.at[2 + i])
        for i, (src, dst) in enumerate(
            (
                (qb, q_out), (kb, k_out), (vb, v_out), (att, att_out),
                (lse, lse_out), (cosb, cos_out), (sinb, sin_out),
            )
        )
    ]
    for copy in outs:
        copy.start()
    for half in range(2):
        got_second_far(half, 2)
    out_dir(0, near[2])
    out_dir(1, near[2])
    last = pltpu.make_async_copy(dot_t, do_out, out_sem.at[2 + len(outs)])
    last.start()
    weight_part(near[2], last=True)
    last.wait()
    for copy in outs:
        copy.wait()
    for copy in started:
        copy.wait_send()
    for t, (_, dst) in enumerate(pairs):
        a2a_wait(t, a2a_send, dst)
    a2a_wait(3, a2a_send, visb)


def backward_kernel(
    q_in, k_in, v_in, do_in, att_in, lse_in, cos_in, sin_in,
    dq_out, dk_out, dv_out,
    qb, kb, vb, dob, attb, lseb, cosb, sinb, dqb, dkb, dvb, dka, dva, kt,
    load_sem, send_sem, recv_sem, own_sem,
):
    me = lax.axis_index("seq")
    samples, tokens, width = q_in.shape
    heads = width // HEAD
    local = tokens // GROUP
    scale = 1.0 / math.sqrt(HEAD)
    scale2 = math.log2(math.e) / math.sqrt(HEAD)
    chunk = 256

    def loads(s):
        return [
            pltpu.make_async_copy(src.at[s], dst.at[s], load_sem.at[s, i])
            for i, (src, dst) in enumerate(
                (
                    (q_in, qb), (k_in, kb), (v_in, vb), (do_in, dob),
                    (att_in, attb), (cos_in, cosb), (sin_in, sinb),
                )
            )
        ]

    shared = pltpu.make_async_copy(lse_in, lseb, load_sem.at[samples, 0])
    shared.start()
    for s in range(samples):
        for copy in loads(s):
            copy.start()
    enter(me)
    shared.wait()

    outs = ((dqb, dq_out), (dkb, dk_out), (dvb, dv_out))

    def item(s, h):
        lanes = slice(h * HEAD, (h + 1) * HEAD)
        row = s * heads + h
        kt[...] = kb[s, :, lanes].astype(F32).T.astype(BF16)
        dka[...] = jnp.zeros_like(dka)
        dva[...] = jnp.zeros_like(dva)

        def one(c, carry):
            place = rows_of(c, chunk)
            queries = qb[s, place, lanes]
            scores = dot(kb[s, :, lanes], queries, NT)
            probs = jnp.exp2(scores * scale2 - lseb[row:row + 1, place])
            into_t = dob[s, lanes, place]
            into_f = into_t.astype(F32)
            into = into_f.T.astype(BF16)
            row_dot = jnp.sum(into_f * attb[s, lanes, place].astype(F32), axis=0, keepdims=True)
            dprobs = dot(vb[s, :, lanes], into_t)
            dscores = (probs * (dprobs - row_dot)).astype(BF16)
            dva[...] += dot(probs.astype(BF16), into)
            dka[...] += dot(dscores, queries)
            dq = (dot(kt[...], dscores).T * scale).astype(BF16).astype(F32)
            dqb[s, place, lanes] = turn(dq, cosb[s, place, :], -sinb[s, place, :]).astype(BF16)
            return carry

        lax.fori_loop(0, tokens // chunk, one, 0)
        dvb[s, :, lanes] = dva[...].astype(BF16)
        dk = (dka[...] * scale).astype(BF16).astype(F32)
        dkb[s, :, lanes] = turn(dk, cosb[s], -sinb[s]).astype(BF16)

    def ship(s, h, count):
        lanes = slice(h * HEAD, (h + count) * HEAD)
        cols = pl.ds(pl.multiple_of(me * width + h * HEAD, HEAD), count * HEAD)
        for t, (src, dst) in enumerate(outs):

            def send_one(off, carry, src=src, dst=dst, t=t):
                target = lax.rem(me + off, GROUP)
                remote(
                    src.at[s, rows_of(target, local), lanes], dst.at[s, :, cols],
                    send_sem.at[t], recv_sem.at[t], target,
                ).start()
                return carry

            lax.fori_loop(1, GROUP, send_one, 0)
            pltpu.make_async_copy(
                src.at[s, rows_of(me, local), lanes], dst.at[s, :, cols], own_sem.at[t]
            ).start()

    for s in range(samples):
        for copy in loads(s):
            copy.wait()
        for h in range(heads):
            item(s, h)
            ship(s, h, 1)

    for t, (src, dst) in enumerate(outs):
        own = dst.at[:, :, pl.ds(0, width)]
        pltpu.make_async_copy(own, own, own_sem.at[t]).wait()
        rest = dst.at[:, :, pl.ds(width, (GROUP - 1) * width)]
        pltpu.make_async_copy(rest, rest, recv_sem.at[t]).wait()
        pltpu.make_async_copy(rest, rest, send_sem.at[t]).wait()


def position_table():
    quarter = HEAD // 8
    frequency = jnp.exp(jnp.arange(quarter, dtype=F32) * (-math.log(100.0) / quarter))
    angle = jnp.arange(GRID, dtype=F32)[:, None] * frequency
    cosine, sine = jnp.cos(angle), jnp.sin(angle)
    none = jnp.zeros((GRID, 2 * quarter), F32)
    rest = jnp.zeros((GRID, HEAD - 4 * quarter), F32)
    row_cos = jnp.concatenate([cosine, cosine, none, rest + 1.0], axis=1)
    col_cos = jnp.concatenate([none, cosine, cosine, rest], axis=1)
    row_sin = jnp.concatenate([-sine, sine, none, rest], axis=1)
    col_sin = jnp.concatenate([none, -sine, sine, rest], axis=1)
    return jnp.concatenate(
        [
            jnp.concatenate([row_cos, row_sin], axis=1),
            jnp.concatenate([col_cos, col_sin], axis=1),
        ],
        axis=0,
    )


def body(query_pre, key_pre, saved_values, out_grad, out_weight, visible):
    samples, local, model = query_pre.shape
    width = model // GROUP
    tokens = local * GROUP
    hbm = pl.BlockSpec(memory_space=pl.ANY)
    vmem = pl.BlockSpec(memory_space=pltpu.VMEM)
    seen = jnp.broadcast_to(visible.reshape(1, samples * local), (8, samples * local))
    item_shape = (samples, tokens, width)
    turned_shape = (samples, width, tokens)
    table_shape = (samples, tokens, HEAD)
    table = position_table()
    dma = pltpu.SemaphoreType.DMA
    q, k, v, do_t, att_t, lse, cosine, sine, partial = pl.pallas_call(
        gather_kernel,
        out_shape=[
            jax.ShapeDtypeStruct(item_shape, BF16),
            jax.ShapeDtypeStruct(item_shape, BF16),
            jax.ShapeDtypeStruct(item_shape, BF16),
            jax.ShapeDtypeStruct(turned_shape, BF16),
            jax.ShapeDtypeStruct(turned_shape, BF16),
            jax.ShapeDtypeStruct((8, tokens), F32),
            jax.ShapeDtypeStruct(table_shape, F32),
            jax.ShapeDtypeStruct(table_shape, F32),
            jax.ShapeDtypeStruct((width, model), BF16),
        ],
        in_specs=[hbm] * 6 + [vmem],
        out_specs=[hbm] * 9,
        scratch_shapes=[
            pltpu.VMEM(item_shape, BF16),
            pltpu.VMEM(item_shape, BF16),
            pltpu.VMEM(item_shape, BF16),
            pltpu.VMEM((samples, tokens, model), BF16),
            pltpu.VMEM((width, model), BF16),
            pltpu.VMEM((GROUP, 8, samples * local), jnp.int32),
            pltpu.VMEM(table_shape, F32),
            pltpu.VMEM(table_shape, F32),
            pltpu.VMEM(turned_shape, BF16),
            pltpu.VMEM(turned_shape, BF16),
            pltpu.VMEM((8, tokens), F32),
            pltpu.VMEM((width, model), F32),
            pltpu.VMEM((2, width, 512), BF16),
            dma((4,)),
            dma((4,)),
            dma((2, 1 + SIDE, 2, 2)),
            dma((2, 1 + SIDE, 2, 2)),
            dma((6,)),
            dma((10,)),
        ],
        compiler_params=pltpu.CompilerParams(
            collective_id=0, has_side_effects=True, vmem_limit_bytes=63 * MIB
        ),
        cost_estimate=pl.CostEstimate(
            flops=24_000_000_000, bytes_accessed=40_000_000, transcendentals=6_000_000
        ),
        name="gather_forward",
    )(query_pre, key_pre, saved_values, out_grad, out_weight, seen, table)
    weight_grad = lax.psum_scatter(partial, "dp", scatter_dimension=0, tiled=True).astype(F32)
    grads = pl.pallas_call(
        backward_kernel,
        out_shape=[jax.ShapeDtypeStruct(query_pre.shape, BF16)] * 3,
        in_specs=[hbm] * 8,
        out_specs=[hbm] * 3,
        scratch_shapes=[
            pltpu.VMEM(item_shape, BF16),
            pltpu.VMEM(item_shape, BF16),
            pltpu.VMEM(item_shape, BF16),
            pltpu.VMEM(turned_shape, BF16),
            pltpu.VMEM(turned_shape, BF16),
            pltpu.VMEM((8, tokens), F32),
            pltpu.VMEM(table_shape, F32),
            pltpu.VMEM(table_shape, F32),
            pltpu.VMEM(item_shape, BF16),
            pltpu.VMEM(item_shape, BF16),
            pltpu.VMEM(item_shape, BF16),
            pltpu.VMEM((tokens, HEAD), F32),
            pltpu.VMEM((tokens, HEAD), F32),
            pltpu.VMEM((HEAD, tokens), BF16),
            dma((samples + 1, 7)),
            dma((3,)),
            dma((3,)),
            dma((3,)),
        ],
        compiler_params=pltpu.CompilerParams(
            collective_id=1, has_side_effects=True, vmem_limit_bytes=60 * MIB
        ),
        cost_estimate=pl.CostEstimate(
            flops=40_000_000_000, bytes_accessed=20_000_000, transcendentals=6_000_000
        ),
        name="backward",
    )(q, k, v, do_t, att_t, lse, cosine, sine)
    return (*grads, weight_grad)


def solution(mesh):
    rows = P("dp", "seq", None)
    return jax.shard_map(
        body,
        mesh=mesh,
        in_specs=(rows, rows, rows, rows, P("seq", None), P("dp", "seq")),
        out_specs=(rows, rows, rows, P(("seq", "dp"), None)),
        check_vma=False,
    )
```

time: 520 us -> 286 us (0.55); the launches traced: 509 us -> 285 us
  Pallas kernels: 0 us -> 261 us
  local copies, waits for them, and re-layouts: 248 us -> 6.71 us
  matrix products: 86.5 us -> 0 us
  waiting for transfers between devices: 74.4 us -> 0.04 us
  other arithmetic: 49.7 us -> 3.09 us
  starting transfers between devices: 35.7 us -> 0.04 us
    pallas_call x0 -> x2, Pallas kernels: none -> 261 us  [the longest x1 199 us: body(): pl.pallas_call(gather_kernel, out_shape=[jax.ShapeDtypeStruct(item_shape,...]
    all_to_all x6 -> x0, waiting for transfers between devices: 73.7 us -> none  [the longest x1 28.9 us: body(): lax.all_to_all(rotated_key_rows, 'seq', split_axis=2, concat_axis=1, tile...]
    dot_general x12 -> x0, matrix products: 66.9 us -> none  [the longest x1 16.7 us: body(): jnp.einsum('snh,snd->hd', attended, grad_all, preferred_element_type=jnp....]
    convert_element_type x4 -> x0, local copies, waits for them, and re-layouts: 61.8 us -> none  [the longest x2 53.4 us: rotate_tokens(): turned.astype(jnp.bfloat16).reshape(seq_count, token_count, model_width)]
    dynamic_slice x10 -> x0, local copies, waits for them, and re-layouts: 57.6 us -> none  [the longest x4 49.4 us: body(): lax.map(lambda operands: attend_backward(*operands), (query_items, key_it...]
    unnamed x33 -> x9, local copies, waits for them, and re-layouts: 43.7 us -> 5.1 us
    all_to_all x6 -> x0, starting transfers between devices: 35.5 us -> none  [the longest x1 7.69 us: body(): lax.all_to_all(rotated_key_rows, 'seq', split_axis=2, concat_axis=1, tile...]
    reshape x6 -> x0, local copies, waits for them, and re-layouts: 24.7 us -> none  [the longest x3 13 us: join_heads(): return tensor.reshape(seq_count, seq_length, owned_width)]
  transfers between devices with their start and end apart: 8 -> 1, of which waited for: 5 -> 0; matrix products, arithmetic and copies ran while one was open for 71% -> 0% of each run, Pallas kernels for 0% -> 22%
where the time goes in v1:
time: 286 us; the launch traced here: 285 us
  Pallas kernels  261 us (91%)
  between operations  14.1 us (5%)
  local copies, waits for them, and re-layouts  6.71 us (2%)
  other arithmetic  3.09 us (1%)
    pallas_call x1, Pallas kernels, body(): pl.pallas_call(gather_kernel, out_shape=[jax.ShapeDtypeStruct(item_shape,...  199 us
    pallas_call x1, Pallas kernels, body(): pl.pallas_call(backward_kernel, out_shape=[jax.ShapeDtypeStruct(query_pre...  61.4 us
  transfers between devices with their start and end apart: 1, of which 0 were waited for; matrix products, arithmetic and copies ran while one was open for 0% of the time, Pallas kernels for 22%

profile of v1, /device:TPU:2, one launch (start us, length us, event | category | flops | bytes accessed | tf_op | source)
XLA Modules:
  0.0 284.6 jit_solution(15167840325070324534)
XLA Ops:
  7.2 0.0 reduce-scatter.2.cloned.1.call-start
  7.2 0.8 broadcast_in_dim.15
  8.0 0.1 fusion
  8.2 0.1 concatenate.10
  8.3 0.1 concatenate.9
  8.4 0.7 pad_maximum_fusion.pos_in
  9.1 0.6 broadcast_in_dim.16.vis_in
  9.7 199.3 %gather_forward.1 = (bf16[2,1024,384]{2,1,0:T(8,128)(2,1)}, bf16[2,1024,384]{2,1,0:T(8,128)(2,1)}, bf16[2,1024,384]{2,1,0:T(8,128)(2,1)}, bf16[2,384,1024]{2,1,0...) custom-call(bf16[2,64,6144]{2,1,0:T(8,128)(2,1)} %q_in.1, ...), custom_call_target="tpu_custom_call" | custom-call | flops 24000000000 | bytes 40000000 | tf_op jit(solution)/shard_map/gather_forward/pallas_call | solution.py:466
  209.0 0.0 reduce-scatter.2.cloned.1.call-update
  209.0 61.4 %backward.1 = (bf16[2,64,6144]{2,1,0:T(8,128)(2,1)}, bf16[2,64,6144]{2,1,0:T(8,128)(2,1)}, bf16[2,64,6144]{2,1,0:T(8,128)(2,1)}) custom-call(bf16[2,1024,384]{2,1,0:T(8,128)(2,1)} %get-tuple-element.16.q_in, bf16[2,1024,384]{2,1,0:T(8,128)(2,1)} %get-tuple-element.17.k_in, bf16[2,1024,384]{2,1,0:T(8,128)(2,1)} %get-tuple-element.18.v_in, ...), custom_call_target="tpu_custom_call" | custom-call | flops 40000000000 | bytes 20000000 | tf_op jit(solution)/shard_map/backward/pallas_call | solution.py:511
  270.3 0.0 copy-start.2
  270.4 0.0 reduce-scatter.2.cloned.1.call-done
  270.4 2.3 convert_element_type.3
  272.7 0.0 copy-done.2
  272.7 0.0 copy-start.1
  272.7 1.1 copy.13
  273.8 0.8 copy-done.1
  274.6 0.0 copy-start
  274.6 1.1 copy.14
  275.8 0.8 copy-done
  276.6 1.1 copy.15
  (4 shorter events, 0.0 us)
Async XLA Ops:
  7.2 263.2 %reduce-scatter.2.cloned.1.call-start = ((), (), s32[]{:S(2)}) async-start(), calls=%async_computation.1 | async-start | bytes 5308416 | tf_op jit(solution)/shard_map/reduce_scatter | solution.py:510
  270.3 2.3 copy-start.2
  272.7 2.0 copy-start.1
  274.6 2.0 copy-start
Sparse Core Ops, SparseCore 0:
  209.1 42.9 reduce-scatter.1

commit v2 on v1

--- a/solution.py
+++ b/solution.py
@@ -39,12 +39,12 @@
         dst_ref=dst,
         send_sem=send,
         recv_sem=recv,
-        device_id={"seq": target},
+        device_id=target if isinstance(target, dict) else {"seq": target},
         device_id_type=MESH,
     )
 
 
-def enter(me):
+def enter(me, rank=None, ranks=1):
     barrier = pltpu.get_barrier_semaphore()
 
     def greet(off, carry):
@@ -53,8 +53,16 @@
         )
         return carry
 
+    def greet_rank(off, carry):
+        pl.semaphore_signal(
+            barrier, inc=1, device_id={"dp": lax.rem(rank + off, ranks)}, device_id_type=MESH
+        )
+        return carry
+
     lax.fori_loop(1, GROUP, greet, 0)
-    pl.semaphore_wait(barrier, GROUP - 1)
+    if ranks > 1:
+        lax.fori_loop(1, ranks, greet_rank, 0)
+    pl.semaphore_wait(barrier, GROUP - 1 + ranks - 1)
 
 
 def rows_of(block, size):
@@ -65,7 +73,7 @@
     q_in, k_in, v_in, g_in, w_in, vis_in, pos_in,
     q_out, k_out, v_out, do_out, att_out, lse_out, cos_out, sin_out, wg_out,
     qb, kb, vb, gb, wb, visb, cosb, sinb, att, dot_t, lse, acc, stage,
-    a2a_send, a2a_recv, ag_send, ag_recv, local_sem, out_sem,
+    a2a_send, a2a_recv, ag_send, ag_recv, local_sem, out_sem, put_sem,
 ):
     me = lax.axis_index("seq")
     px, py = lax.rem(me, SIDE), lax.div(me, SIDE)
@@ -245,15 +253,19 @@
         place = rows_of(row, part)
         dot_t[s, :, place] = dot(wb[...], gb[s, place, :], NT).astype(BF16)
 
-    tile = stage.shape[2]
+    tile = stage.shape[4]
 
     def weight_part(row, first=False, last=False):
         place = rows_of(row, part)
 
-        def put(j, slot):
-            return pltpu.make_async_copy(
-                stage.at[slot], wg_out.at[:, rows_of(j, tile)], out_sem.at[slot]
-            )
+        def puts(j, slot):
+            return [
+                pltpu.make_async_copy(
+                    stage.at[slot, :, core], wg_out.at[core, :, :, rows_of(j, tile)],
+                    put_sem.at[slot, core],
+                )
+                for core in range(2)
+            ]
 
         def one(j, carry):
             cols = rows_of(j, tile)
@@ -267,10 +279,12 @@
 
                 @pl.when(j >= 2)
                 def _():
-                    put(j - 2, slot).wait()
-
-                stage[slot] = total.astype(BF16)
-                put(j, slot).start()
+                    for copy in puts(j - 2, slot):
+                        copy.wait()
+
+                stage[slot] = total.astype(BF16).reshape(stage.shape[1:])
+                for copy in puts(j, slot):
+                    copy.start()
             else:
                 acc[:, cols] = total
             return carry
@@ -279,7 +293,8 @@
         lax.fori_loop(0, steps, one, 0)
         if last:
             for j in (steps - 2, steps - 1):
-                put(j, j % 2).wait()
+                for copy in puts(j, j % 2):
+                    copy.wait()
 
     near = [lax.rem(py + d, SIDE) for d in range(SIDE)]
 
@@ -335,12 +350,16 @@
 
 
 def backward_kernel(
-    q_in, k_in, v_in, do_in, att_in, lse_in, cos_in, sin_in,
-    dq_out, dk_out, dv_out,
+    ranks,
+    q_in, k_in, v_in, do_in, att_in, lse_in, cos_in, sin_in, wg_in,
+    dq_out, dk_out, dv_out, wg_out,
     qb, kb, vb, dob, attb, lseb, cosb, sinb, dqb, dkb, dvb, dka, dva, kt,
-    load_sem, send_sem, recv_sem, own_sem,
+    wga, wgs, wgz, wgf,
+    load_sem, send_sem, recv_sem, own_sem, wg_send, wg_recv, wg_sem,
 ):
-    me = lax.axis_index("seq")
+    me, rank = lax.axis_index("seq"), lax.axis_index("dp")
+    levels = ranks // 2
+    level, core = lax.div(rank, 2), lax.rem(rank, 2)
     samples, tokens, width = q_in.shape
     heads = width // HEAD
     local = tokens // GROUP
@@ -364,7 +383,56 @@
     for s in range(samples):
         for copy in loads(s):
             copy.start()
-    enter(me)
+    own_part = pltpu.make_async_copy(wg_in.at[core], wga, wg_sem.at[0])
+    own_part.start()
+    enter(me, rank, ranks)
+
+    to_core = remote(
+        wg_in.at[1 - core], wgs, wg_send.at[0], wg_recv.at[0], {"dp": level * 2 + 1 - core}
+    )
+    to_core.start()
+
+    def to_level(off):
+        target = lax.rem(level + off, levels)
+        return remote(
+            wga.at[target], wgz.at[off - 1], wg_send.at[off], wg_recv.at[off],
+            {"dp": target * 2 + core},
+        )
+
+    done = pltpu.make_async_copy(wgf, wg_out, wg_sem.at[1])
+    model = wga.shape[2]
+    piece = 512
+
+    def add_cores():
+        own_part.wait()
+        to_core.wait_recv()
+
+        def one(c, carry):
+            cols = rows_of(c, piece)
+            wga[:, :, cols] = (
+                wga[:, :, cols].astype(F32) + wgs[:, :, cols].astype(F32)
+            ).astype(BF16)
+            return carry
+
+        lax.fori_loop(0, model // piece, one, 0)
+        for off in range(1, levels):
+            to_level(off).start()
+
+    def add_levels():
+        for off in range(1, levels):
+            to_level(off).wait_recv()
+
+        def one(c, carry):
+            cols = rows_of(c, piece)
+            total = wga[level, :, cols].astype(F32)
+            for off in range(1, levels):
+                total += wgz[off - 1, :, cols].astype(F32)
+            wgf[:, cols] = total
+            return carry
+
+        lax.fori_loop(0, model // piece, one, 0)
+        done.start()
+
     shared.wait()
 
     outs = ((dqb, dq_out), (dkb, dk_out), (dvb, dv_out))
@@ -422,6 +490,9 @@
         for h in range(heads):
             item(s, h)
             ship(s, h, 1)
+            if (s, h) == (0, 0):
+                add_cores()
+    add_levels()
 
     for t, (src, dst) in enumerate(outs):
         own = dst.at[:, :, pl.ds(0, width)]
@@ -429,6 +500,10 @@
         rest = dst.at[:, :, pl.ds(width, (GROUP - 1) * width)]
         pltpu.make_async_copy(rest, rest, recv_sem.at[t]).wait()
         pltpu.make_async_copy(rest, rest, send_sem.at[t]).wait()
+    to_core.wait_send()
+    for off in range(1, levels):
+        to_level(off).wait_send()
+    done.wait()
 
 
 def position_table():
@@ -461,6 +536,8 @@
     item_shape = (samples, tokens, width)
     turned_shape = (samples, width, tokens)
     table_shape = (samples, tokens, HEAD)
+    ranks = lax.axis_size("dp")
+    partial_shape = (2, ranks // 2, width // ranks, model)
     table = position_table()
     dma = pltpu.SemaphoreType.DMA
     q, k, v, do_t, att_t, lse, cosine, sine, partial = pl.pallas_call(
@@ -474,7 +551,7 @@
             jax.ShapeDtypeStruct((8, tokens), F32),
             jax.ShapeDtypeStruct(table_shape, F32),
             jax.ShapeDtypeStruct(table_shape, F32),
-            jax.ShapeDtypeStruct((width, model), BF16),
+            jax.ShapeDtypeStruct(partial_shape, BF16),
         ],
         in_specs=[hbm] * 6 + [vmem],
         out_specs=[hbm] * 9,
@@ -491,13 +568,14 @@
             pltpu.VMEM(turned_shape, BF16),
             pltpu.VMEM((8, tokens), F32),
             pltpu.VMEM((width, model), F32),
-            pltpu.VMEM((2, width, 512), BF16),
+            pltpu.VMEM((2, ranks // 2, 2, width // ranks, 512), BF16),
             dma((4,)),
             dma((4,)),
             dma((2, 1 + SIDE, 2, 2)),
             dma((2, 1 + SIDE, 2, 2)),
             dma((6,)),
             dma((10,)),
+            dma((2, 2)),
         ],
         compiler_params=pltpu.CompilerParams(
             collective_id=0, has_side_effects=True, vmem_limit_bytes=63 * MIB
@@ -507,12 +585,12 @@
         ),
         name="gather_forward",
     )(query_pre, key_pre, saved_values, out_grad, out_weight, seen, table)
-    weight_grad = lax.psum_scatter(partial, "dp", scatter_dimension=0, tiled=True).astype(F32)
-    grads = pl.pallas_call(
-        backward_kernel,
-        out_shape=[jax.ShapeDtypeStruct(query_pre.shape, BF16)] * 3,
-        in_specs=[hbm] * 8,
-        out_specs=[hbm] * 3,
+    return pl.pallas_call(
+        functools.partial(backward_kernel, ranks),
+        out_shape=[jax.ShapeDtypeStruct(query_pre.shape, BF16)] * 3
+        + [jax.ShapeDtypeStruct(partial_shape[2:], F32)],
+        in_specs=[hbm] * 9,
+        out_specs=[hbm] * 4,
         scratch_shapes=[
             pltpu.VMEM(item_shape, BF16),
             pltpu.VMEM(item_shape, BF16),
@@ -528,10 +606,17 @@
             pltpu.VMEM((tokens, HEAD), F32),
             pltpu.VMEM((tokens, HEAD), F32),
             pltpu.VMEM((HEAD, tokens), BF16),
+            pltpu.VMEM(partial_shape[1:], BF16),
+            pltpu.VMEM(partial_shape[1:], BF16),
+            pltpu.VMEM((ranks // 2 - 1, *partial_shape[2:]), BF16),
+            pltpu.VMEM(partial_shape[2:], F32),
             dma((samples + 1, 7)),
             dma((3,)),
             dma((3,)),
             dma((3,)),
+            dma((ranks // 2,)),
+            dma((ranks // 2,)),
+            dma((2,)),
         ],
         compiler_params=pltpu.CompilerParams(
             collective_id=1, has_side_effects=True, vmem_limit_bytes=60 * MIB
@@ -540,8 +625,7 @@
             flops=40_000_000_000, bytes_accessed=20_000_000, transcendentals=6_000_000
         ),
         name="backward",
-    )(q, k, v, do_t, att_t, lse, cosine, sine)
-    return (*grads, weight_grad)
+    )(q, k, v, do_t, att_t, lse, cosine, sine, partial)
 
 
 def solution(mesh):

time: 286 us -> 275 us (0.962)
  between operations: 14.1 us -> 0.7 us
  Pallas kernels: 261 us -> 264 us
    pallas_call x1, Pallas kernels: 61.4 us -> 64.9 us  [body(): pl.pallas_call(functools.partial(backward_kernel, ranks), out_shape=[jax....]
    unnamed x9 -> x10, local copies, waits for them, and re-layouts: 5.1 us -> 7.64 us
  transfers between devices with their start and end apart: 1 -> 0, of which waited for: 0 -> 0; matrix products, arithmetic and copies ran while one was open for 0% -> 0% of each run, Pallas kernels for 22% -> 0%
where the time goes in v2:
time: 275 us
  Pallas kernels  264 us (96%)
  local copies, waits for them, and re-layouts  9.26 us (3%)
    pallas_call x1, Pallas kernels, body(): pl.pallas_call(gather_kernel, out_shape=[jax.ShapeDtypeStruct(item_shape,...  199 us
    pallas_call x1, Pallas kernels, body(): pl.pallas_call(functools.partial(backward_kernel, ranks), out_shape=[jax....  64.9 us
    unnamed x10, local copies, waits for them, and re-layouts  7.64 us

profile of v2, /device:TPU:2, one launch (start us, length us, event | category | flops | bytes accessed | tf_op | source)
XLA Modules:
  0.0 275.0 jit_solution(412010157171455950)
XLA Ops:
  0.6 0.8 broadcast_in_dim.15
  1.4 0.6 broadcast_in_dim.16.vis_in
  2.0 0.1 fusion
  2.2 0.1 concatenate.9
  2.3 0.1 concatenate.10
  2.4 0.7 pad_maximum_fusion.pos_in
  3.1 199.3 %gather_forward.1 = (bf16[2,1024,384]{2,1,0:T(8,128)(2,1)}, bf16[2,1024,384]{2,1,0:T(8,128)(2,1)}, bf16[2,1024,384]{2,1,0:T(8,128)(2,1)}, bf16[2,384,1024]{2,1,0...) custom-call(bf16[2,64,6144]{2,1,0:T(8,128)(2,1)} %q_in.1, ...), custom_call_target="tpu_custom_call" | custom-call | flops 24000000000 | bytes 40000000 | tf_op jit(solution)/shard_map/gather_forward/pallas_call | solution.py:543
  202.5 64.9 %backward.1 = (bf16[2,64,6144]{2,1,0:T(8,128)(2,1)}, bf16[2,64,6144]{2,1,0:T(8,128)(2,1)}, bf16[2,64,6144]{2,1,0:T(8,128)(2,1)}, f32[48,6144]{1,0:T(8,128)}) custom-call(bf16[2,1024,384]{2,1,0:T(8,128)(2,1)} %get-tuple-element.13.q_in, bf16[2,1024,384]{2,1,0:T(8,128)(2,1)} %get-tuple-element.14.k_in, bf16[2,1024,384]{2,1,0:T(8,128)(2,1)} %get-tuple-element.15.v_in, ...), custom_call_target="tpu_custom_call" | custom-call | flops 40000000000 | bytes 20000000 | tf_op jit(solution)/shard_map/backward/pallas_call | solution.py:588
  267.4 0.0 copy-start.1
  267.4 2.8 %copy.14 = bf16[2,64,6144]{2,1,0:T(8,128)(2,1)} copy(bf16[2,64,6144]{2,1,0:T(8,128)(2,1)} %get-tuple-element.29) | data formatting | bytes 3145728
  270.2 0.0 copy-done.1
  270.2 0.0 copy-start
  270.2 1.1 copy.15
  271.3 0.8 copy-done
  272.2 0.0 copy-start.2
  272.2 1.1 copy.16
  273.3 0.7 copy-done.2
  274.0 1.0 copy.17
  (4 shorter events, 0.0 us)
Async XLA Ops:
  267.4 2.8 %copy-start.1 = (bf16[2,64,6144]{2,1,0:T(8,128)(2,1)S(1)}, bf16[2,64,6144]{2,1,0:T(8,128)(2,1)}, u32[]{:S(2)}) copy-start(bf16[2,64,6144]{2,1,0:T(8,128)(2,1)} %get-tuple-element.30) | copy-start | bytes 4718596
  270.2 2.0 copy-start
  272.2 1.8 copy-start.2

commit v3 on v2

--- a/solution.py
+++ b/solution.py
@@ -568,7 +568,7 @@
             pltpu.VMEM(turned_shape, BF16),
             pltpu.VMEM((8, tokens), F32),
             pltpu.VMEM((width, model), F32),
-            pltpu.VMEM((2, ranks // 2, 2, width // ranks, 512), BF16),
+            pltpu.VMEM((2, ranks // 2, 2, width // ranks, 1024), BF16),
             dma((4,)),
             dma((4,)),
             dma((2, 1 + SIDE, 2, 2)),

time: 275 us -> 272 us (0.989)
  Pallas kernels: 264 us -> 260 us
    pallas_call x1, Pallas kernels: 199 us -> 195 us  [body(): pl.pallas_call(gather_kernel, out_shape=[jax.ShapeDtypeStruct(item_shape,...]
where the time goes in v3:
time: 272 us; the launch traced here: 271 us
  Pallas kernels  260 us (96%)
  local copies, waits for them, and re-layouts  9.26 us (3%)
    pallas_call x1, Pallas kernels, body(): pl.pallas_call(gather_kernel, out_shape=[jax.ShapeDtypeStruct(item_shape,...  195 us
    pallas_call x1, Pallas kernels, body(): pl.pallas_call(functools.partial(backward_kernel, ranks), out_shape=[jax....  64.9 us
    unnamed x10, local copies, waits for them, and re-layouts  7.64 us

profile of v3, /device:TPU:2, one launch (start us, length us, event | category | flops | bytes accessed | tf_op | source)
XLA Modules:
  0.0 270.9 jit_solution(943536086637716561)
XLA Ops:
  0.6 0.8 broadcast_in_dim.15
  1.4 0.6 broadcast_in_dim.16.vis_in
  2.0 0.1 fusion
  2.2 0.1 concatenate.9
  2.3 0.1 concatenate.10
  2.4 0.7 pad_maximum_fusion.pos_in
  3.1 195.2 %gather_forward.1 = (bf16[2,1024,384]{2,1,0:T(8,128)(2,1)}, bf16[2,1024,384]{2,1,0:T(8,128)(2,1)}, bf16[2,1024,384]{2,1,0:T(8,128)(2,1)}, bf16[2,384,1024]{2,1,0...) custom-call(bf16[2,64,6144]{2,1,0:T(8,128)(2,1)} %q_in.1, ...), custom_call_target="tpu_custom_call" | custom-call | flops 24000000000 | bytes 40000000 | tf_op jit(solution)/shard_map/gather_forward/pallas_call | solution.py:543
  198.3 64.9 %backward.1 = (bf16[2,64,6144]{2,1,0:T(8,128)(2,1)}, bf16[2,64,6144]{2,1,0:T(8,128)(2,1)}, bf16[2,64,6144]{2,1,0:T(8,128)(2,1)}, f32[48,6144]{1,0:T(8,128)}) custom-call(bf16[2,1024,384]{2,1,0:T(8,128)(2,1)} %get-tuple-element.13.q_in, bf16[2,1024,384]{2,1,0:T(8,128)(2,1)} %get-tuple-element.14.k_in, bf16[2,1024,384]{2,1,0:T(8,128)(2,1)} %get-tuple-element.15.v_in, ...), custom_call_target="tpu_custom_call" | custom-call | flops 40000000000 | bytes 20000000 | tf_op jit(solution)/shard_map/backward/pallas_call | solution.py:588
  263.3 0.0 copy-start.1
  263.3 2.8 %copy.14 = bf16[2,64,6144]{2,1,0:T(8,128)(2,1)} copy(bf16[2,64,6144]{2,1,0:T(8,128)(2,1)} %get-tuple-element.29) | data formatting | bytes 3145728
  266.1 0.0 copy-done.1
  266.1 0.0 copy-start
  266.1 1.1 copy.15
  267.2 0.8 copy-done
  268.1 0.0 copy-start.2
  268.1 1.1 copy.16
  269.2 0.7 copy-done.2
  269.9 1.0 copy.17
  (4 shorter events, 0.0 us)
Async XLA Ops:
  263.3 2.8 %copy-start.1 = (bf16[2,64,6144]{2,1,0:T(8,128)(2,1)S(1)}, bf16[2,64,6144]{2,1,0:T(8,128)(2,1)}, u32[]{:S(2)}) copy-start(bf16[2,64,6144]{2,1,0:T(8,128)(2,1)} %get-tuple-element.30) | copy-start | bytes 4718596
  266.1 2.0 copy-start
  268.1 1.8 copy-start.2

commit v4 on v3

--- a/solution.py
+++ b/solution.py
@@ -3,6 +3,7 @@
 
 import jax
 import jax.numpy as jnp
+import numpy as np
 from jax import lax
 from jax.experimental import pallas as pl
 from jax.experimental.pallas import tpu as pltpu
@@ -354,7 +355,7 @@
     q_in, k_in, v_in, do_in, att_in, lse_in, cos_in, sin_in, wg_in,
     dq_out, dk_out, dv_out, wg_out,
     qb, kb, vb, dob, attb, lseb, cosb, sinb, dqb, dkb, dvb, dka, dva, kt,
-    wga, wgs, wgz, wgf,
+    wga, wgs,
     load_sem, send_sem, recv_sem, own_sem, wg_send, wg_recv, wg_sem,
 ):
     me, rank = lax.axis_index("seq"), lax.axis_index("dp")
@@ -395,11 +396,11 @@
     def to_level(off):
         target = lax.rem(level + off, levels)
         return remote(
-            wga.at[target], wgz.at[off - 1], wg_send.at[off], wg_recv.at[off],
+            wga.at[target], wg_out.at[off], wg_send.at[off], wg_recv.at[off],
             {"dp": target * 2 + core},
         )
 
-    done = pltpu.make_async_copy(wgf, wg_out, wg_sem.at[1])
+    own_share = pltpu.make_async_copy(wga.at[level], wg_out.at[0], wg_sem.at[1])
     model = wga.shape[2]
     piece = 512
 
@@ -415,23 +416,9 @@
             return carry
 
         lax.fori_loop(0, model // piece, one, 0)
+        own_share.start()
         for off in range(1, levels):
             to_level(off).start()
-
-    def add_levels():
-        for off in range(1, levels):
-            to_level(off).wait_recv()
-
-        def one(c, carry):
-            cols = rows_of(c, piece)
-            total = wga[level, :, cols].astype(F32)
-            for off in range(1, levels):
-                total += wgz[off - 1, :, cols].astype(F32)
-            wgf[:, cols] = total
-            return carry
-
-        lax.fori_loop(0, model // piece, one, 0)
-        done.start()
 
     shared.wait()
 
@@ -492,7 +479,6 @@
             ship(s, h, 1)
             if (s, h) == (0, 0):
                 add_cores()
-    add_levels()
 
     for t, (src, dst) in enumerate(outs):
         own = dst.at[:, :, pl.ds(0, width)]
@@ -502,28 +488,20 @@
         pltpu.make_async_copy(rest, rest, send_sem.at[t]).wait()
     to_core.wait_send()
     for off in range(1, levels):
-        to_level(off).wait_send()
-    done.wait()
+        to_level(off).wait()
+    own_share.wait()
 
 
 def position_table():
     quarter = HEAD // 8
-    frequency = jnp.exp(jnp.arange(quarter, dtype=F32) * (-math.log(100.0) / quarter))
-    angle = jnp.arange(GRID, dtype=F32)[:, None] * frequency
-    cosine, sine = jnp.cos(angle), jnp.sin(angle)
-    none = jnp.zeros((GRID, 2 * quarter), F32)
-    rest = jnp.zeros((GRID, HEAD - 4 * quarter), F32)
-    row_cos = jnp.concatenate([cosine, cosine, none, rest + 1.0], axis=1)
-    col_cos = jnp.concatenate([none, cosine, cosine, rest], axis=1)
-    row_sin = jnp.concatenate([-sine, sine, none, rest], axis=1)
-    col_sin = jnp.concatenate([none, -sine, sine, rest], axis=1)
-    return jnp.concatenate(
-        [
-            jnp.concatenate([row_cos, row_sin], axis=1),
-            jnp.concatenate([col_cos, col_sin], axis=1),
-        ],
-        axis=0,
-    )
+    frequency = 100.0 ** (-np.arange(quarter) / quarter)
+    angle = np.arange(GRID)[:, None] * frequency
+    cosine, sine = np.cos(angle), np.sin(angle)
+    none = np.zeros((GRID, 2 * quarter))
+    rest = np.zeros((GRID, HEAD - 4 * quarter))
+    row = np.concatenate([cosine, cosine, none, rest + 1.0, -sine, sine, none, rest], axis=1)
+    col = np.concatenate([none, cosine, cosine, rest, none, -sine, sine, rest], axis=1)
+    return jnp.asarray(np.concatenate([row, col], axis=0), F32)
 
 
 def body(query_pre, key_pre, saved_values, out_grad, out_weight, visible):
@@ -585,10 +563,10 @@
         ),
         name="gather_forward",
     )(query_pre, key_pre, saved_values, out_grad, out_weight, seen, table)
-    return pl.pallas_call(
+    *grads, shares = pl.pallas_call(
         functools.partial(backward_kernel, ranks),
         out_shape=[jax.ShapeDtypeStruct(query_pre.shape, BF16)] * 3
-        + [jax.ShapeDtypeStruct(partial_shape[2:], F32)],
+        + [jax.ShapeDtypeStruct(partial_shape[1:], BF16)],
         in_specs=[hbm] * 9,
         out_specs=[hbm] * 4,
         scratch_shapes=[
@@ -608,8 +586,6 @@
             pltpu.VMEM((HEAD, tokens), BF16),
             pltpu.VMEM(partial_shape[1:], BF16),
             pltpu.VMEM(partial_shape[1:], BF16),
-            pltpu.VMEM((ranks // 2 - 1, *partial_shape[2:]), BF16),
-            pltpu.VMEM(partial_shape[2:], F32),
             dma((samples + 1, 7)),
             dma((3,)),
             dma((3,)),
@@ -626,6 +602,7 @@
         ),
         name="backward",
     )(q, k, v, do_t, att_t, lse, cosine, sine, partial)
+    return (*grads, jnp.sum(shares.astype(F32), axis=0))
 
 
 def solution(mesh):

time: 272 us -> 272 us (level)
  local copies, waits for them, and re-layouts: 9.26 us -> 6.45 us
    reduce_sum x0 -> x1, other arithmetic: none -> 3.26 us  [body(): return (*grads, jnp.sum(shares.astype(F32), axis=0))]
    unnamed x10 -> x9, local copies, waits for them, and re-layouts: 7.64 us -> 5.1 us
where the time goes in v4:
time: 272 us; the launch traced here: 271 us
  Pallas kernels  260 us (96%)
  local copies, waits for them, and re-layouts  6.45 us (2%)
  other arithmetic  3.26 us (1%)
    pallas_call x1, Pallas kernels, body(): pl.pallas_call(gather_kernel, out_shape=[jax.ShapeDtypeStruct(item_shape,...  195 us
    pallas_call x1, Pallas kernels, body(): pl.pallas_call(functools.partial(backward_kernel, ranks), out_shape=[jax....  64.9 us

profile of v4, /device:TPU:2, one launch (start us, length us, event | category | flops | bytes accessed | tf_op | source)
XLA Modules:
  0.0 270.6 jit_solution(11232047967683174335)
XLA Ops:
  0.6 0.8 broadcast_in_dim.7
  1.4 0.6 broadcast_in_dim.8.vis_in
  2.0 195.3 %gather_forward.1 = (bf16[2,1024,384]{2,1,0:T(8,128)(2,1)}, bf16[2,1024,384]{2,1,0:T(8,128)(2,1)}, bf16[2,1024,384]{2,1,0:T(8,128)(2,1)}, bf16[2,384,1024]{2,1,0...) custom-call(bf16[2,64,6144]{2,1,0:T(8,128)(2,1)} %q_in.1, ...), custom_call_target="tpu_custom_call" | custom-call | flops 24000000000 | bytes 40000000 | tf_op jit(solution)/shard_map/gather_forward/pallas_call | solution.py:521
  197.3 64.9 %backward.1 = (bf16[2,64,6144]{2,1,0:T(8,128)(2,1)}, bf16[2,64,6144]{2,1,0:T(8,128)(2,1)}, bf16[2,64,6144]{2,1,0:T(8,128)(2,1)}, bf16[4,48,6144]{2,1,0:T(8,128)(2,1)}) custom-call(bf16[2,1024,384]{2,1,0:T(8,128)(2,1)} %get-tuple-element.17.q_in, bf16[2,1024,384]{2,1,0:T(8,128)(2,1)} %get-tuple-element.18.k_in, bf16[2,1024,384]{2,1,0:T(8,128)(2,1)} %get-tuple-element.19.v_in, ...), custom_call_target="tpu_custom_call" | custom-call | flops 40000000000 | bytes 20000000 | tf_op jit(solution)/shard_map/backward/pallas_call | solution.py:566
  262.2 0.0 copy-start.2
  262.2 3.3 %convert_reduce_fusion = f32[48,6144]{1,0:T(8,128)} fusion(bf16[4,48,6144]{2,1,0:T(8,128)(2,1)} %get-tuple-element.29), kind=kLoop, calls=%fused_computation | loop fusion | flops 2064384 | bytes 3538944 | tf_op jit(solution)/shard_map/reduce_sum | solution.py:605
  265.5 0.0 copy-done.2
  265.5 0.0 copy-start.1
  265.5 1.1 copy.14
  266.6 0.8 copy-done.1
  267.5 0.0 copy-start
  267.5 1.1 copy.15
  268.6 0.8 copy-done
  269.4 1.1 copy.16
Async XLA Ops:
  262.2 3.3 %copy-start.2 = (bf16[2,64,6144]{2,1,0:T(8,128)(2,1)S(1)}, bf16[2,64,6144]{2,1,0:T(8,128)(2,1)}, u32[]{:S(2)}) copy-start(bf16[2,64,6144]{2,1,0:T(8,128)(2,1)} %get-tuple-element.34) | copy-start | bytes 4718596
  265.5 2.0 copy-start.1
  267.5 2.0 copy-start
